TPU v7x, 256 devices: a whole 4x4x8 slice. The times are simulated.
256 devices in a mesh: seq: 16 (over y, x), head: 8 (over z), dp: 2 (over core).
Axes of the slice: x: 4, y: 4, z: 8, core: 2. Of those that a mesh axis runs over, the one named last changes fastest.
Arguments:
- hidden: bfloat16 [8192, 2560], P(('dp', 'seq', 'head')), parts along dimension 0, may hold values from -6 to 6
- x_input: bfloat16 [8192, 5120], P(('dp', 'seq', 'head')), parts along dimension 0, may hold values from -6 to 6
- grad_out: bfloat16 [8192, 5120], P(('dp', 'seq', 'head')), parts along dimension 0, may hold values from -6 to 6
- bc_weight: bfloat16 [2560, 256], replicated, may hold values from -0.01953125 to 0.01953125
- dt_weight: bfloat16 [2560, 80], replicated, may hold values from -0.125 to 0.125
- dt_bias: float32 [80], replicated, may hold values from -3 to -2
- a_log: float32 [80], replicated, may hold values from -10 to -1.6
- d_skip: float32 [80], replicated, may hold values from 0.5 to 1.5
Outputs:
- mixer_out: bfloat16 [8192, 5120], P(('dp', 'seq', 'head')), parts along dimension 0
- grad_x: bfloat16 [8192, 5120], P(('dp', 'seq', 'head')), parts along dimension 0
- grad_hidden: bfloat16 [8192, 2560], P(('dp', 'seq', 'head')), parts along dimension 0
- grad_bc_weight: float32 [5120, 256], P('dp'), parts along dimension 0
- grad_dt_weight: float32 [5120, 80], P('dp'), parts along dimension 0
- param_grads: float32 [6, 80], P('dp'), parts along dimension 0
There are 2 independent parts, one for each index of `dp`. A program takes and returns all parts, laid end to end along the dimension named above; an argument that names none is the same for every part. Nothing has to cross between parts.
All inputs are finite; a program needn't handle non-finite values.
Results may differ from a plain program's by a relative error of at most 0.02.
Values may be sent and summed in bfloat16 or wider, within the bound.
No kernel may reach another device: no remote copies, remote signals or barrier semaphores. Data moves between devices by JAX's collectives and lax.ppermute only.
A program may use at most 128 MiB of HBM per device.

v0:
```python
import jax
import jax.numpy as jnp
from jax import lax
from jax.sharding import PartitionSpec as P

Q = 256
precise = lax.Precision.HIGHEST


def prefix_2(value, axis, combine, identity):
    devices, place = (lax.axis_size(axis), lax.axis_index(axis))
    everything = jax.tree.map(
        lambda part, kind: lax.all_gather(part.astype(kind), axis),
        value,
        (jnp.bfloat16, jnp.bfloat16),
    )
    start = jax.tree.map(
        lambda part, zero: jnp.broadcast_to(jnp.asarray(zero, part.dtype), part.shape),
        value,
        identity,
    )

    def step(k, before):
        reached = k < place
        new = combine(
            before, jax.tree.map(lambda part, own: part[k].astype(own.dtype), everything, value)
        )
        return jax.tree.map(lambda a, b: jnp.where(reached, a, b), new, before)

    return lax.fori_loop(0, devices, step, start)


def prefix_3(part, axis, combine, identity):
    count = lax.axis_size(axis)
    place = lax.axis_index(axis)
    ahead = count - 1 - place
    gathered = jax.tree.map(lambda a: lax.all_gather(a, axis), part)
    state = jax.tree.map(lambda a, e: jnp.zeros_like(a) + jnp.asarray(e, a.dtype), part, identity)

    def one(step, state):
        source = count - 1 - step
        return combine(
            state, jax.tree.map(lambda a: lax.dynamic_index_in_dim(a, source, 0, False), gathered)
        )

    return lax.fori_loop(0, ahead, one, state)


def span_scan(x_heads, step_size, b_rows, c_rows, neg_rate, state_in):
    length = x_heads.shape[0]
    blocks = length // Q
    heads_here = x_heads.shape[1]
    head_width = x_heads.shape[2]
    states = b_rows.shape[1]
    causal = (jnp.arange(Q)[:, None] >= jnp.arange(Q)[None, :])[:, :, None]

    def span_advance(carry, block):
        x_block, step_block, b_block, c_block = block
        running = jnp.cumsum(step_block * neg_rate[None, :], axis=0)
        scores = jnp.dot(c_block, b_block.T, precision=precise)
        spread = running[:, None, :] - running[None, :, :]
        decay = jnp.where(causal, jnp.exp(jnp.where(causal, spread, 0.0)), 0.0)
        scaled_x = x_block * step_block[:, :, None]
        inner = jnp.einsum("qkh,khp->qhp", decay * scores[:, :, None], scaled_x, precision=precise)
        carried = (
            jnp.einsum("qn,hnp->qhp", c_block, carry, precision=precise)
            * jnp.exp(running)[:, :, None]
        )
        total = running[-1]
        weights_end = jnp.exp(total[None, :] - running)
        fresh = jnp.einsum(
            "kn,khp->hnp", b_block, scaled_x * weights_end[:, :, None], precision=precise
        )
        return (jnp.exp(total)[:, None, None] * carry + fresh, inner + carried)

    pieces = (
        x_heads.reshape(blocks, Q, heads_here, head_width),
        step_size.reshape(blocks, Q, heads_here),
        b_rows.reshape(blocks, Q, states),
        c_rows.reshape(blocks, Q, states),
    )
    state_out, outputs = lax.scan(jax.checkpoint(span_advance), state_in, pieces)
    return (outputs.reshape(length, heads_here, head_width), state_out)


def mixer_local(x_heads, raw_step, b_rows, c_rows, log_decay, skip_gain, step_bias, state_in):
    step_size = jax.nn.softplus(raw_step + step_bias[None, :])
    neg_rate = -jnp.exp(log_decay)
    mixed, state_out = span_scan(x_heads, step_size, b_rows, c_rows, neg_rate, state_in)
    return (mixed + skip_gain[None, :, None] * x_heads, state_out)


def device_totals(x_heads, step_size, b_rows, c_rows, grad_heads, neg_rate):
    length = x_heads.shape[0]
    heads_here = x_heads.shape[1]
    head_width = x_heads.shape[2]
    states = b_rows.shape[1]
    blocks = length // Q

    def device_advance(carry, block):
        prefix, state_sum, adjoint_sum = carry
        x_block, step_block, b_block, c_block, grad_block = block
        running = jnp.cumsum(step_block * neg_rate[None, :], axis=0)
        total = running[-1]
        weights_end = jnp.exp(total[None, :] - running)
        scaled_x = x_block * step_block[:, :, None]
        fresh = jnp.einsum(
            "kn,khp->hnp", b_block, scaled_x * weights_end[:, :, None], precision=precise
        )
        state_sum = jnp.exp(total)[:, None, None] * state_sum + fresh
        reach = jnp.exp(prefix[None, :] + running)
        adjoint_sum = adjoint_sum + jnp.einsum(
            "qn,qhp->hnp", c_block, grad_block * reach[:, :, None], precision=precise
        )
        return ((prefix + total, state_sum, adjoint_sum), None)

    pieces = (
        x_heads.reshape(blocks, Q, heads_here, head_width),
        step_size.reshape(blocks, Q, heads_here),
        b_rows.reshape(blocks, Q, states),
        c_rows.reshape(blocks, Q, states),
        grad_heads.reshape(blocks, Q, heads_here, head_width),
    )
    start = (
        jnp.zeros((heads_here,), jnp.float32),
        jnp.zeros((heads_here, states, head_width), jnp.float32),
        jnp.zeros((heads_here, states, head_width), jnp.float32),
    )
    (prefix, state_sum, adjoint_sum), unused = lax.scan(device_advance, start, pieces)
    return (jnp.exp(prefix), state_sum, adjoint_sum)


def combine_pairs(earlier, later):
    return (earlier[0] * later[0], later[0][:, None, None] * earlier[1] + later[1])


def per_device(hidden, x_input, grad_out, bc_weight, dt_weight, dt_bias, a_log, d_skip):
    groups = lax.axis_size("head")
    head_index = lax.axis_index("head")
    heads_all = dt_weight.shape[1]
    heads_local = heads_all // groups
    head_width = x_input.shape[1] // heads_all
    states = bc_weight.shape[1] // 2
    proj_bc = jnp.dot(hidden, bc_weight, preferred_element_type=jnp.float32).astype(jnp.bfloat16)
    proj_dt = jnp.dot(hidden, dt_weight, preferred_element_type=jnp.float32).astype(jnp.bfloat16)
    x_local, raw_local, grad_local = (
        lax.all_to_all(x_input, "head", split_axis=1, concat_axis=0, tiled=True),
        lax.all_to_all(proj_dt, "head", split_axis=1, concat_axis=0, tiled=True),
        lax.all_to_all(grad_out, "head", split_axis=1, concat_axis=0, tiled=True),
    )
    bc_local = lax.all_gather(proj_bc, "head", axis=0, tiled=True)
    length = x_local.shape[0]
    x_heads = x_local.astype(jnp.float32).reshape(length, heads_local, head_width)
    grad_heads = grad_local.astype(jnp.float32).reshape(length, heads_local, head_width)
    raw_step = raw_local.astype(jnp.float32)
    b_rows = bc_local[:, :states].astype(jnp.float32)
    c_rows = bc_local[:, states:].astype(jnp.float32)
    offset = head_index * heads_local
    bias_local = lax.dynamic_slice_in_dim(dt_bias, offset, heads_local)
    log_local = lax.dynamic_slice_in_dim(a_log, offset, heads_local)
    skip_local = lax.dynamic_slice_in_dim(d_skip, offset, heads_local)
    step_size = jax.nn.softplus(raw_step + bias_local[None, :])
    neg_rate = -jnp.exp(log_local)
    decay_all, state_sum, adjoint_sum = device_totals(
        x_heads, step_size, b_rows, c_rows, grad_heads, neg_rate
    )
    identity = (
        jnp.ones((heads_local,), jnp.float32),
        jnp.zeros((heads_local, states, head_width), jnp.float32),
    )
    state_in = prefix_2((decay_all, state_sum), "seq", combine_pairs, identity)[1]
    state_grad = prefix_3((decay_all, adjoint_sum), "seq", combine_pairs, identity)[1]

    def forward(x_arg, raw_arg, b_arg, c_arg, log_arg, skip_arg, bias_arg):
        return mixer_local(x_arg, raw_arg, b_arg, c_arg, log_arg, skip_arg, bias_arg, state_in)

    (mixed, state_end), pullback = jax.vjp(
        forward, x_heads, raw_step, b_rows, c_rows, log_local, skip_local, bias_local
    )
    grad_xs, grad_raw, grad_b, grad_c, grad_alog, grad_skip, grad_bias = pullback(
        (grad_heads, state_grad)
    )
    out_local = mixed.reshape(length, heads_local * head_width).astype(jnp.bfloat16)
    gradx_local = grad_xs.reshape(length, heads_local * head_width).astype(jnp.bfloat16)
    step_local = grad_raw.astype(jnp.bfloat16)
    mixer_out, grad_x, d_step = (
        lax.all_to_all(out_local, "head", split_axis=0, concat_axis=1, tiled=True),
        lax.all_to_all(gradx_local, "head", split_axis=0, concat_axis=1, tiled=True),
        lax.all_to_all(step_local, "head", split_axis=0, concat_axis=1, tiled=True),
    )
    d_bc = lax.psum_scatter(
        jnp.concatenate([grad_b, grad_c], axis=1).astype(jnp.bfloat16),
        "head",
        scatter_dimension=0,
        tiled=True,
    )
    grad_hidden = (
        jnp.dot(d_bc, bc_weight.T, preferred_element_type=jnp.float32)
        + jnp.dot(d_step, dt_weight.T, preferred_element_type=jnp.float32)
    ).astype(jnp.bfloat16)
    seq_total = length * lax.axis_size("seq")
    weight_bc = jnp.dot(hidden.T, d_bc, preferred_element_type=jnp.float32) / seq_total
    weight_dt = jnp.dot(hidden.T, d_step, preferred_element_type=jnp.float32) / seq_total
    stacked = jnp.stack([grad_bias, grad_alog, grad_skip]) / seq_total
    param_local = lax.dynamic_update_slice(
        jnp.zeros((3, heads_all), jnp.float32), stacked, (0, offset)
    )
    grad_bc_weight, grad_dt_weight, param_grads = lax.psum(
        (weight_bc, weight_dt, param_local), ("seq", "head")
    )
    return (mixer_out, grad_x, grad_hidden, grad_bc_weight, grad_dt_weight, param_grads)


def solution(mesh):
    in_specs = (
        P(("dp", "seq", "head"), None),
        P(("dp", "seq", "head"), None),
        P(("dp", "seq", "head"), None),
        P(),
        P(),
        P(),
        P(),
        P(),
    )
    out_specs = (
        P(("dp", "seq", "head"), None),
        P(("dp", "seq", "head"), None),
        P(("dp", "seq", "head"), None),
        P("dp", None),
        P("dp", None),
        P("dp", None),
    )
    return jax.shard_map(
        per_device, mesh=mesh, in_specs=in_specs, out_specs=out_specs, check_vma=False
    )
```

profile of v0, /device:TPU:0, one launch (start us, length us, event | category | flops | bytes accessed | tf_op | source)
XLA Modules:
  0.0 757.0 jit_solution(9546356608684292287)
XLA Ops:
  9.5 6.7 all-to-all-start.1
  19.9 4.0 all-to-all-done.1
  23.9 3.4 all-to-all-start
  27.4 27.6 %all_gather.23 = bf16[256,256]{1,0:T(8,128)(2,1)S(1)} all-gather(bf16[32,256]{1,0:T(8,128)(2,1)S(1)} %convolution_convert_fusion), channel_id=1, replica_groups=mesh['seq'=16,'head'=8,'dp'=2] {'head'}, dimensions={0}, use_global_device_ids=true | all-gather | bytes 147456 | tf_op jit(solution)/shard_map/all_gather | solution.py:151
  57.0 6.1 all-to-all-start.3
  77.8 3.5 multiply_reduce_fusion
  82.8 2.6 fusion.62
  91.4 20.9 %all-gather.2 = bf16[16,1,10]{2,1,0:T(2,128)(2,1)S(1)} all-gather(bf16[1,1,10]{2,1,0:T(2,128)(2,1)S(1)} %bitcast.278), channel_id=1, replica_groups=mesh['seq'=16,'head'=8,'dp'=2] {'seq'}, dimensions={0}, use_global_device_ids=true | all-gather | bytes 340 | tf_op jit(solution)/shard_map/all_gather | solution.py:13
  112.3 21.2 %all-gather.3 = f32[16,1,10]{2,1,0:T(1,128)} all-gather(f32[1,1,10]{2,1,0:T(1,128)} %bitcast.276), channel_id=1, replica_groups=mesh['seq'=16,'head'=8,'dp'=2] {'seq'}, dimensions={0}, use_global_device_ids=true | all-gather | bytes 680 | tf_op jit(solution)/shard_map/all_gather | solution.py:37
  139.1 22.0 %while.21 = (s32[]{:T(128)}, f32[10,128,64]{2,1,0:T(8,128)S(1)}, s32[]{:T(128)}, bf16[16,10]{1,0:T(8,128)(2,1)S(1)}, bf16[16,10,128,64]{2,3,1,0:T(8,128)(2,1)}, /*index=5*/s32[]{:T(128)}, s32[]{:T(128)}) while((s32[]{:T(128)}, f32[10,128,64]{2,1,0:T(8,128)S(1)}, s32[]{:T(128)}, bf16[16,10]{1,0:T(8,128)(2,1)S(1)}, ...), condition=%wide.region_3.4_spmd.clone, body=%wide.region_2.3_spmd.clone.sunk | while | flops 409614 | bytes 1474765 | solution.py:30
  161.1 41.3 %all-gather.9.cloned.1.call-done = f32[160,128,64]{1,2,0:T(8,128)} async-done(((f32[10,128,64]{1,2,0:T(8,128)}), f32[160,128,64]{1,2,0:T(8,128)}) %all-gather.9.cloned.1.call-update) | async-done | bytes 5242896 | tf_op jit(solution)/shard_map/all_gather | solution.py:37
  202.5 57.5 %while.20 = (s32[]{:T(128)}, f32[10,128,64]{2,1,0:T(8,128)S(1)}, s32[]{:T(128)}, f32[16,10]{1,0:T(8,128)}, f32[16,10,128,64]{2,3,1,0:T(8,128)}, /*index=5*/s32[]{:T(128)}, s32[]{:T(128)}, s32[]{:T(128)}, s32[]{:T(128)}) while((s32[]{:T(128)}, f32[10,128,64]{2,1,0:T(8,128)S(1)}, s32[]{:T(128)}, f32[16,10]{1,0:T(8,128)}, ...), condition=%wide.region_5.6_spmd, body=%wide.region_4.5_spmd.sunk | while | flops 163846 | bytes 2294027 | solution.py:46
  268.0 3.0 copy.262
  271.0 3.0 copy.251
  278.4 5.8 fusion.19
  284.3 3.9 multiply_reduce_fusion.3
  293.2 2.7 reduce-window.42
  296.2 2.3 broadcast_multiply_fusion
  302.8 7.0 all-to-all-start.5
  310.7 6.8 all-to-all-done.5
  318.8 28.1 %reduce-scatter.4.cloned.1.call-done = bf16[32,256]{1,0:T(8,128)(2,1)} async-done(((bf16[256,256]{1,0:T(8,128)(2,1)}), bf16[32,256]{1,0:T(8,128)(2,1)}) %reduce-scatter.4.cloned.1.call-update) | async-done | bytes 16400
  346.9 2.7 fusion.1
  350.5 3.6 broadcast_multiply_fusion.1
  354.8 6.0 fusion.48
  360.9 2.4 copy.238
  364.6 2.4 copy.252
  368.3 2.6 add_convert_fusion
  370.9 4.4 all-to-all-start.2
  375.6 14.4 %all-to-all-done.2 = bf16[8,32,640]{2,1,0:T(8,128)(2,1)S(1)} async-done(((bf16[8,32,640]{2,1,0:T(8,128)(2,1)}), bf16[8,32,640]{2,1,0:T(8,128)(2,1)S(1)}, u32[]{:S(2)}, u32[]{:S(2)}) %all-to-all-start.2) | async-done | bytes 327712 | tf_op jit(solution)/shard_map/all_to_all | solution.py:187
  390.0 3.4 all-to-all-start.4
  393.6 349.3 %psum.23 = f32[3,80]{1,0:T(4,128)} all-reduce(f32[3,80]{1,0:T(4,128)S(1)} %dynamic_update_slice.19), channel_id=1, replica_groups=mesh['seq'=16,'head'=8,'dp'=2] {'seq','head'}, use_global_device_ids=true, to_apply=%region_25.26 | all-reduce | flops 240 | bytes 1920 | tf_op jit(solution)/shard_map/psum | solution.py:208
  745.9 3.3 copy.269
  (349 shorter events, 146.1 us)
Async XLA Ops:
  7.2 9.0 %copy-start = (bf16[2560,256]{1,0:T(8,128)(2,1)S(1)}, bf16[2560,256]{1,0:T(8,128)(2,1)}, u32[]{:S(2)}) copy-start(bf16[2560,256]{1,0:T(8,128)(2,1)} %param.15) | copy-start | bytes 3932164
  7.2 47.8 %copy-start.45 = (f32[80]{0:T(128)S(1)}, f32[80]{0:T(128)}, u32[]{:S(2)}) copy-start(f32[80]{0:T(128)} %param.17) | copy-start | bytes 964
  7.2 47.9 %copy-start.14 = (bf16[32,5120]{1,0:T(8,128)(2,1)S(1)}, bf16[32,5120]{1,0:T(8,128)(2,1)}, u32[]{:S(2)}) copy-start(bf16[32,5120]{1,0:T(8,128)(2,1)} %param.14) | copy-start | bytes 983044
  9.5 14.5 %all-to-all-start.1 = ((bf16[8,2,160]{2,1,0:T(2,128)(2,1)}), bf16[8,2,160]{2,1,0:T(2,128)(2,1)S(1)}, u32[]{:S(2)}, u32[]{:S(2)}) async-start(bf16[8,2,160]{2,1,0:T(2,128)(2,1)} %reshape.399), calls=%async_computation.1 | async-start | bytes 16384 | tf_op jit(solution)/shard_map/all_to_all | solution.py:148
  18.2 46.4 %copy-start.34 = (f32[10]{0:T(128)}, f32[10]{0:T(128)S(1)}, u32[]{:S(2)}) copy-start(f32[10]{0:T(128)S(1)} %fusion.113) | copy-start | bytes 124
  23.9 33.0 %all-to-all-start = ((bf16[32,8,640]{2,0,1:T(8,128)(2,1)}), bf16[32,8,640]{2,0,1:T(8,128)(2,1)S(1)}, u32[]{:S(2)}, u32[]{:S(2)}) async-start(bf16[32,8,640]{2,0,1:T(8,128)(2,1)} %bitcast.236), calls=%async_computation | async-start | bytes 655360 | tf_op jit(solution)/shard_map/all_to_all | solution.py:147
  55.1 9.6 %copy-start.36 = (f32[10]{0:T(128)}, f32[10]{0:T(128)S(1)}, u32[]{:S(2)}) copy-start(f32[10]{0:T(128)S(1)} %dynamic_slice.73) | copy-start | bytes 124
  55.9 8.7 %copy-start.15 = (bf16[8,10,32]{2,1,0:T(8,128)(2,1)}, bf16[8,10,32]{2,1,0:T(8,128)(2,1)S(1)}, u32[]{:S(2)}) copy-start(bf16[8,10,32]{2,1,0:T(8,128)(2,1)S(1)} %reshape.400) | copy-start | bytes 15364
  56.0 7.1 copy-start.22
  57.0 7.7 %copy-start.1 = (bf16[32,8,640]{2,0,1:T(8,128)(2,1)}, bf16[32,8,640]{2,0,1:T(8,128)(2,1)S(1)}, u32[]{:S(2)}) copy-start(bf16[32,8,640]{2,0,1:T(8,128)(2,1)S(1)} %all-to-all-done) | copy-start | bytes 983044
  57.0 20.9 %all-to-all-start.3 = ((bf16[32,8,640]{2,0,1:T(8,128)(2,1)}), bf16[32,8,640]{2,0,1:T(8,128)(2,1)}, u32[]{:S(2)}, u32[]{:S(2)}) async-start(bf16[32,8,640]{2,0,1:T(8,128)(2,1)} %bitcast.235), calls=%async_computation.3 | async-start | bytes 655360 | tf_op jit(solution)/shard_map/all_to_all | solution.py:149
  63.0 76.1 %all-gather.7.cloned.1.call-start = ((), (), s32[]{:S(2)}) async-start(), calls=%async_computation.7 | async-start | bytes 2785280 | tf_op jit(solution)/shard_map/all_gather | solution.py:13
  85.5 117.0 %all-gather.9.cloned.1.call-start = ((), (), s32[]{:S(2)}) async-start(), calls=%async_computation.8 | async-start | bytes 5570560 | tf_op jit(solution)/shard_map/all_gather | solution.py:37
  90.5 176.4 %copy-start.3 = (f32[256,128]{1,0:T(8,128)}, f32[256,128]{1,0:T(8,128)S(1)}, u32[]{:S(2)}) copy-start(f32[256,128]{1,0:T(8,128)S(1)} %get-tuple-element.368) | copy-start | bytes 393220
  261.7 9.3 %copy-start.38 = (f32[10]{0:T(128)}, f32[10]{0:T(128)S(1)}, u32[]{:S(2)}) copy-start(f32[10]{0:T(128)S(1)} %slice_bitcast_fusion) | copy-start | bytes 124
  278.4 5.8 copy-start.28
  278.4 5.8 copy-start.32
  298.5 19.2 %copy-start.2 = (bf16[32,2560]{1,0:T(8,128)(2,1)S(1)}, bf16[32,2560]{1,0:T(8,128)(2,1)}, u32[]{:S(2)}) copy-start(bf16[32,2560]{1,0:T(8,128)(2,1)} %param.12) | copy-start | bytes 491524
  302.8 14.7 %all-to-all-start.5 = ((bf16[8,2,160]{2,1,0:T(2,128)(2,1)}), bf16[8,2,160]{2,1,0:T(2,128)(2,1)S(1)}, u32[]{:S(2)}, u32[]{:S(2)}) async-start(bf16[8,2,160]{2,1,0:T(2,128)(2,1)} %reshape.401), calls=%async_computation.5 | async-start | bytes 16384 | tf_op jit(solution)/shard_map/all_to_all | solution.py:189
  309.8 37.1 %reduce-scatter.4.cloned.1.call-start = ((), (), s32[]{:S(2)}) async-start(), calls=%async_computation.9 | async-start | bytes 147456
  310.7 435.2 %all-reduce.4.cloned.1.call-start = ((), (), s32[]{:S(2)}) async-start(), calls=%async_computation.10 | async-start | bytes 6881280 | tf_op jit(solution)/shard_map/psum | solution.py:208
  317.7 32.0 %copy-start.18 = (bf16[32,80]{0,1:T(8,128)(2,1)}, bf16[32,80]{0,1:T(8,128)(2,1)S(1)}, u32[]{:S(2)}) copy-start(bf16[32,80]{0,1:T(8,128)(2,1)S(1)} %all_to_all.80) | copy-start | bytes 15364
  318.8 30.8 %copy-start.46 = (f32[80]{0:T(128)S(1)}, f32[80]{0:T(128)}, u32[]{:S(2)}) copy-start(f32[80]{0:T(128)} %param.19) | copy-start | bytes 964
  366.9 8.3 %copy-start.29 = (f32[640]{0:T(1024)S(1)}, f32[640]{0:T(1024)}, u32[]{:S(2)}) copy-start(f32[640]{0:T(1024)} %get-tuple-element.533) | copy-start | bytes 7684
  367.0 8.5 %copy-start.42 = (f32[10]{0:T(128)S(1)}, f32[10]{0:T(128)}, u32[]{:S(2)}) copy-start(f32[10]{0:T(128)} %get-tuple-element.542) | copy-start | bytes 124
  367.0 8.5 %copy-start.44 = (f32[80]{0:T(128)S(1)}, f32[80]{0:T(128)}, u32[]{:S(2)}) copy-start(f32[80]{0:T(128)} %param.18) | copy-start | bytes 964
  368.3 25.2 %copy-start.40 = (f32[10]{0:T(128)S(1)}, f32[10]{0:T(128)}, u32[]{:S(2)}) copy-start(f32[10]{0:T(128)} %get-tuple-element.530) | copy-start | bytes 124
  368.3 374.6 %copy-start.24 = (bf16[32,256]{1,0:T(8,128)(2,1)S(1)}, bf16[32,256]{1,0:T(8,128)(2,1)}, u32[]{:S(2)}) copy-start(bf16[32,256]{1,0:T(8,128)(2,1)} %reduce-scatter.4.cloned.1.call-done) | copy-start | bytes 49156
  368.3 375.1 %copy-start.7 = (bf16[2560,80]{0,1:T(8,128)(2,1)S(1)}, bf16[2560,80]{0,1:T(8,128)(2,1)}, u32[]{:S(2)}) copy-start(bf16[2560,80]{0,1:T(8,128)(2,1)} %param.16) | copy-start | bytes 1228804
  368.3 375.1 %copy-start.19 = (bf16[32,80]{0,1:T(8,128)(2,1)S(1)}, bf16[32,80]{0,1:T(8,128)(2,1)}, u32[]{:S(2)}) copy-start(bf16[32,80]{0,1:T(8,128)(2,1)} %copy-done.18) | copy-start | bytes 15364
  370.9 19.1 %all-to-all-start.2 = ((bf16[8,32,640]{2,1,0:T(8,128)(2,1)}), bf16[8,32,640]{2,1,0:T(8,128)(2,1)S(1)}, u32[]{:S(2)}, u32[]{:S(2)}) async-start(bf16[8,32,640]{2,1,0:T(8,128)(2,1)} %get-tuple-element.546), calls=%async_computation.2 | async-start | bytes 655360 | tf_op jit(solution)/shard_map/all_to_all | solution.py:187
  390.0 355.1 %all-to-all-start.4 = ((bf16[8,32,640]{2,1,0:T(8,128)(2,1)}), bf16[8,32,640]{2,1,0:T(8,128)(2,1)S(1)}, u32[]{:S(2)}, u32[]{:S(2)}) async-start(bf16[8,32,640]{2,1,0:T(8,128)(2,1)} %get-tuple-element.545), calls=%async_computation.4 | async-start | bytes 655360 | tf_op jit(solution)/shard_map/all_to_all | solution.py:188
  (25 other events, 93.7 us)
Sparse Core Ops, SparseCore 0:
  85.6 52.9 all-gather.6
  141.6 60.7 all-gather.8
  313.7 33.1 reduce-scatter.3
  353.9 237.4 all-reduce.3
where the time goes:
time: 768 us; the launch traced here: 757 us
  blocking collectives  419 us (55%)
  local copies, waits for them, and re-layouts  124 us (16%)
  waiting for transfers between devices  94.7 us (12%)
  matrix products  38.5 us (5%)
  other arithmetic  32.8 us (4%)
  starting transfers between devices  31.3 us (4%)
  between operations  14.9 us (2%)
    psum x1, blocking collectives, per_device(): lax.psum((weight_bc, weight_dt, param_local), ('seq', 'head'))  349 us
    dynamic_slice x30, local copies, waits for them, and re-layouts, one(): lax.dynamic_index_in_dim(a, source, 0, False)  44 us
    all_gather x1, waiting for transfers between devices, prefix_3(): gathered = jax.tree.map(lambda a: lax.all_gather(a, axis), part)  41.3 us
    unnamed x5, waiting for transfers between devices  28.1 us
    all_gather x1, blocking collectives, per_device(): bc_local = lax.all_gather(proj_bc, 'head', axis=0, tiled=True)  27.6 us
    all_gather x1, blocking collectives, prefix_3(): gathered = jax.tree.map(lambda a: lax.all_gather(a, axis), part)  21.2 us
    all_gather x1, blocking collectives, prefix_2(): lax.all_gather(part.astype(kind), axis)  20.9 us
    dynamic_slice x32, local copies, waits for them, and re-layouts, step(): part[k].astype(own.dtype)  18.6 us
  transfers between devices with their start and end apart: 10, of which 5 were waited for; matrix products, arithmetic and copies ran while one was open for 10% of the time, Pallas kernels for 0%

commit v1 on v0

--- a/solution.py
+++ b/solution.py
@@ -148,7 +148,12 @@
         lax.all_to_all(proj_dt, "head", split_axis=1, concat_axis=0, tiled=True),
         lax.all_to_all(grad_out, "head", split_axis=1, concat_axis=0, tiled=True),
     )
-    bc_local = lax.all_gather(proj_bc, "head", axis=0, tiled=True)
+    ring = [proj_bc]
+    for hop in range(7):
+        ring.append(lax.ppermute(ring[-1], "head", [(dev, (dev + 1) % 8) for dev in range(8)]))
+    bc_local = jnp.roll(
+        jnp.concatenate(ring[::-1], axis=0), (lax.axis_index("head") + 1) * ring[0].shape[0], axis=0
+    )
     length = x_local.shape[0]
     x_heads = x_local.astype(jnp.float32).reshape(length, heads_local, head_width)
     grad_heads = grad_local.astype(jnp.float32).reshape(length, heads_local, head_width)

time: 768 us -> 777 us (1.012)
  blocking collectives: 419 us -> 392 us
  starting transfers between devices: 31.3 us -> 48.9 us
  waiting for transfers between devices: 94.7 us -> 106 us
    all_gather x1 -> x0, blocking collectives: 27.6 us -> none  [per_device(): bc_local = lax.all_gather(proj_bc, 'head', axis=0, tiled=True)]
    ppermute x0 -> x7, waiting for transfers between devices: none -> 23.6 us  [per_device(): lax.ppermute(ring[-1], 'head', [(dev, (dev + 1) % 8) for dev in range(8)])]
    all_gather x1, waiting for transfers between devices: 41.3 us -> 25.6 us  [prefix_3(): gathered = jax.tree.map(lambda a: lax.all_gather(a, axis), part)]
    all_gather x1, starting transfers between devices: 0.04 us -> 11 us  [prefix_3(): gathered = jax.tree.map(lambda a: lax.all_gather(a, axis), part)]
    unnamed x107 -> x132, local copies, waits for them, and re-layouts: 8.48 us -> 18.1 us
  transfers between devices with their start and end apart: 10 -> 17, of which waited for: 5 -> 11; matrix products, arithmetic and copies ran while one was open for 10% -> 11% of each run, Pallas kernels for 0% -> 0%
where the time goes in v1:
time: 777 us; the launch traced here: 764 us
  blocking collectives  392 us (50%)
  local copies, waits for them, and re-layouts  131 us (17%)
  waiting for transfers between devices  106 us (14%)
  starting transfers between devices  48.9 us (6%)
  matrix products  39.5 us (5%)
  other arithmetic  30.1 us (4%)
  between operations  14.9 us (2%)
    psum x1, blocking collectives, per_device(): lax.psum((weight_bc, weight_dt, param_local), ('seq', 'head'))  350 us
    dynamic_slice x30, local copies, waits for them, and re-layouts, one(): lax.dynamic_index_in_dim(a, source, 0, False)  44 us
    unnamed x5, waiting for transfers between devices  28.1 us
    all_gather x1, waiting for transfers between devices, prefix_3(): gathered = jax.tree.map(lambda a: lax.all_gather(a, axis), part)  25.6 us
    ppermute x7, waiting for transfers between devices, per_device(): lax.ppermute(ring[-1], 'head', [(dev, (dev + 1) % 8) for dev in range(8)])  23.6 us
    all_gather x1, blocking collectives, prefix_3(): gathered = jax.tree.map(lambda a: lax.all_gather(a, axis), part)  21.2 us
    all_gather x1, blocking collectives, prefix_2(): lax.all_gather(part.astype(kind), axis)  20.9 us
    dynamic_slice x32, local copies, waits for them, and re-layouts, step(): part[k].astype(own.dtype)  18.6 us
  transfers between devices with their start and end apart: 17, of which 11 were waited for; matrix products, arithmetic and copies ran while one was open for 11% of the time, Pallas kernels for 0%

profile of v1, /device:TPU:0, one launch (start us, length us, event | category | flops | bytes accessed | tf_op | source)
XLA Modules:
  0.0 763.8 jit_solution(8158561481899301002)
XLA Ops:
  9.5 6.7 all-to-all-start.1
  24.0 5.3 all-to-all-start
  32.3 5.4 collective-permute-done.1
  37.9 4.7 collective-permute-done.2
  42.8 4.8 collective-permute-done.3
  48.4 4.2 collective-permute-done.4
  53.3 4.4 collective-permute-done.5
  72.2 6.7 all-to-all-start.3
  83.3 6.8 all-to-all-done.3
  90.1 3.5 multiply_reduce_fusion
  95.2 2.8 fusion.62
  98.0 11.0 %all-gather.9.cloned.1.call-start = ((), (), s32[]{:S(2)}) async-start(), calls=%async_computation.8 | async-start | bytes 5570560 | tf_op jit(solution)/shard_map/all_gather | solution.py:37
  110.6 2.9 fusion.56
  114.3 20.9 %all-gather.2 = bf16[16,1,10]{2,1,0:T(2,128)(2,1)S(1)} all-gather(bf16[1,1,10]{2,1,0:T(2,128)(2,1)S(1)} %bitcast.279), channel_id=1, replica_groups=mesh['seq'=16,'head'=8,'dp'=2] {'seq'}, dimensions={0}, use_global_device_ids=true | all-gather | bytes 340 | tf_op jit(solution)/shard_map/all_gather | solution.py:13
  135.3 21.2 %all-gather.3 = f32[16,1,10]{2,1,0:T(1,128)} all-gather(f32[1,1,10]{2,1,0:T(1,128)S(1)} %bitcast.277), channel_id=1, replica_groups=mesh['seq'=16,'head'=8,'dp'=2] {'seq'}, dimensions={0}, use_global_device_ids=true | all-gather | bytes 680 | tf_op jit(solution)/shard_map/all_gather | solution.py:37
  162.1 22.0 %while.21 = (s32[]{:T(128)}, f32[10,128,64]{2,1,0:T(8,128)S(1)}, s32[]{:T(128)}, bf16[16,10]{1,0:T(8,128)(2,1)S(1)}, bf16[16,10,128,64]{2,3,1,0:T(8,128)(2,1)}, /*index=5*/s32[]{:T(128)}, s32[]{:T(128)}) while((s32[]{:T(128)}, f32[10,128,64]{2,1,0:T(8,128)S(1)}, s32[]{:T(128)}, bf16[16,10]{1,0:T(8,128)(2,1)S(1)}, ...), condition=%wide.region_3.4_spmd.clone, body=%wide.region_2.3_spmd.clone.sunk | while | flops 409614 | bytes 1474765 | solution.py:30
  184.0 25.6 %all-gather.9.cloned.1.call-done = f32[160,128,64]{1,2,0:T(8,128)} async-done(((f32[10,128,64]{1,2,0:T(8,128)}), f32[160,128,64]{1,2,0:T(8,128)}) %all-gather.9.cloned.1.call-update) | async-done | bytes 5242896 | tf_op jit(solution)/shard_map/all_gather | solution.py:37
  209.7 57.4 %while.20 = (s32[]{:T(128)}, f32[10,128,64]{2,1,0:T(8,128)S(1)}, s32[]{:T(128)}, f32[16,10]{1,0:T(8,128)}, f32[16,10,128,64]{2,3,1,0:T(8,128)}, /*index=5*/s32[]{:T(128)}, s32[]{:T(128)}, s32[]{:T(128)}, s32[]{:T(128)}) while((s32[]{:T(128)}, f32[10,128,64]{2,1,0:T(8,128)S(1)}, s32[]{:T(128)}, f32[16,10]{1,0:T(8,128)}, ...), condition=%wide.region_5.6_spmd, body=%wide.region_4.5_spmd.sunk | while | flops 163846 | bytes 2294027 | solution.py:46
  275.0 3.0 copy.262
  278.1 3.0 copy.251
  285.5 5.8 fusion.19
  291.3 3.9 multiply_reduce_fusion.3
  309.1 7.0 all-to-all-start.5
  317.1 6.8 all-to-all-done.5
  325.2 28.1 %reduce-scatter.4.cloned.1.call-done = bf16[32,256]{1,0:T(8,128)(2,1)} async-done(((bf16[256,256]{1,0:T(8,128)(2,1)}), bf16[32,256]{1,0:T(8,128)(2,1)}) %reduce-scatter.4.cloned.1.call-update) | async-done | bytes 16400
  356.9 3.6 broadcast_multiply_fusion.1
  361.1 6.1 fusion.48
  377.2 4.4 all-to-all-start.2
  381.8 14.5 %all-to-all-done.2 = bf16[8,32,640]{2,1,0:T(8,128)(2,1)S(1)} async-done(((bf16[8,32,640]{2,1,0:T(8,128)(2,1)}), bf16[8,32,640]{2,1,0:T(8,128)(2,1)S(1)}, u32[]{:S(2)}, u32[]{:S(2)}) %all-to-all-start.2) | async-done | bytes 327712 | tf_op jit(solution)/shard_map/all_to_all | solution.py:192
  396.3 3.4 all-to-all-start.4
  399.9 349.9 %psum.23 = f32[3,80]{1,0:T(4,128)} all-reduce(f32[3,80]{1,0:T(4,128)S(1)} %dynamic_update_slice.19), channel_id=1, replica_groups=mesh['seq'=16,'head'=8,'dp'=2] {'seq','head'}, use_global_device_ids=true, to_apply=%region_25.26 | all-reduce | flops 240 | bytes 1920 | tf_op jit(solution)/shard_map/psum | solution.py:213
  752.7 3.3 copy.269
  (388 shorter events, 167.9 us)
Async XLA Ops:
  9.5 14.5 %all-to-all-start.1 = ((bf16[8,2,160]{2,1,0:T(2,128)(2,1)}), bf16[8,2,160]{2,1,0:T(2,128)(2,1)S(1)}, u32[]{:S(2)}, u32[]{:S(2)}) async-start(bf16[8,2,160]{2,1,0:T(2,128)(2,1)} %reshape.399), calls=%async_computation.1 | async-start | bytes 16384 | tf_op jit(solution)/shard_map/all_to_all | solution.py:148
  17.4 40.7 %copy-start.20 = (bf16[32,256]{1,0:T(8,128)(2,1)}, bf16[32,256]{1,0:T(8,128)(2,1)S(1)}, u32[]{:S(2)}) copy-start(bf16[32,256]{1,0:T(8,128)(2,1)S(1)} %convolution_convert_fusion) | copy-start | bytes 49156
  17.5 12.0 %collective-permute-start = (bf16[32,256]{1,0:T(8,128)(2,1)S(1)}, bf16[32,256]{1,0:T(8,128)(2,1)S(1)}, u32[]{:S(2)}, u32[]{:S(2)}) collective-permute-start(bf16[32,256]{1,0:T(8,128)(2,1)S(1)} %convolution_convert_fusion), channel_id=1, source_target_pairs={{0,2},{2,4},{4,6},{6,8},{8,10},{10,12},{12,14},{14,0},{1,3},{3,5},... | collective-permute-start | bytes 49160 | tf_op jit(solution)/shard_map/ppermute | solution.py:153
  20.3 37.9 %copy-start.41 = (f32[10]{0:T(128)}, f32[10]{0:T(128)S(1)}, u32[]{:S(2)}) copy-start(f32[10]{0:T(128)S(1)} %fusion.115) | copy-start | bytes 124
  21.0 37.1 %copy-start.43 = (f32[10]{0:T(128)}, f32[10]{0:T(128)S(1)}, u32[]{:S(2)}) copy-start(f32[10]{0:T(128)S(1)} %dynamic_slice.77) | copy-start | bytes 124
  24.0 48.2 %all-to-all-start = ((bf16[32,8,640]{2,0,1:T(8,128)(2,1)}), bf16[32,8,640]{2,0,1:T(8,128)(2,1)}, u32[]{:S(2)}, u32[]{:S(2)}) async-start(bf16[32,8,640]{2,0,1:T(8,128)(2,1)} %bitcast.236), calls=%async_computation | async-start | bytes 655360 | tf_op jit(solution)/shard_map/all_to_all | solution.py:147
  29.3 28.8 %copy-start.17 = (bf16[8,10,32]{2,1,0:T(8,128)(2,1)}, bf16[8,10,32]{2,1,0:T(8,128)(2,1)S(1)}, u32[]{:S(2)}) copy-start(bf16[8,10,32]{2,1,0:T(8,128)(2,1)S(1)} %reshape.400) | copy-start | bytes 15364
  29.5 28.7 %copy-start.24 = (f32[256,10]{0,1:T(8,128)}, f32[256,10]{0,1:T(8,128)S(1)}, u32[]{:S(2)}) copy-start(f32[256,10]{0,1:T(8,128)S(1)} %reshape.372) | copy-start | bytes 30724
  29.5 28.7 %copy-start.31 = (bf16[32,256]{1,0:T(8,128)(2,1)}, bf16[32,256]{1,0:T(8,128)(2,1)S(1)}, u32[]{:S(2)}) copy-start(bf16[32,256]{1,0:T(8,128)(2,1)S(1)} %collective-permute-done) | copy-start | bytes 49156
  29.5 8.2 %collective-permute-start.1 = (bf16[32,256]{1,0:T(8,128)(2,1)S(1)}, bf16[32,256]{1,0:T(8,128)(2,1)S(1)}, u32[]{:S(2)}, u32[]{:S(2)}) collective-permute-start(bf16[32,256]{1,0:T(8,128)(2,1)S(1)} %collective-permute-done), channel_id=1, source_target_pairs={{0,2},{2,4},{4,6},{6,8},{8,10},{10,12},{12,14},{14,0},{1,3},{3,5},... | collective-permute-start | bytes 49160 | tf_op jit(solution)/shard_map/ppermute | solution.py:153
  37.7 4.9 collective-permute-start.2
  42.7 4.9 collective-permute-start.3
  47.6 4.9 collective-permute-start.4
  52.6 5.1 collective-permute-start.5
  57.6 7.4 collective-permute-start.6
  72.2 17.9 %all-to-all-start.3 = ((bf16[32,8,640]{2,0,1:T(8,128)(2,1)}), bf16[32,8,640]{2,0,1:T(8,128)(2,1)S(1)}, u32[]{:S(2)}, u32[]{:S(2)}) async-start(bf16[32,8,640]{2,0,1:T(8,128)(2,1)} %bitcast.251), calls=%async_computation.3 | async-start | bytes 655360 | tf_op jit(solution)/shard_map/all_to_all | solution.py:149
  78.9 83.1 %all-gather.7.cloned.1.call-start = ((), (), s32[]{:S(2)}) async-start(), calls=%async_computation.7 | async-start | bytes 2785280 | tf_op jit(solution)/shard_map/all_gather | solution.py:13
  98.0 16.1 %copy-start.22 = (f32[2,8,2,128]{3,1,2,0:T(8,128)S(1)}, f32[2,8,2,128]{3,1,2,0:T(8,128)}, u32[]{:S(2)}) copy-start(f32[2,8,2,128]{3,1,2,0:T(8,128)} %copy-done.21) | copy-start | bytes 49156
  98.0 37.3 %copy-start.48 = (f32[10]{0:T(128)S(1)}, f32[10]{0:T(128)}, u32[]{:S(2)}) copy-start(f32[10]{0:T(128)} %get-tuple-element.506) | copy-start | bytes 124
  98.0 111.6 %all-gather.9.cloned.1.call-start = ((), (), s32[]{:S(2)}) async-start(), calls=%async_computation.8 | async-start | bytes 5570560 | tf_op jit(solution)/shard_map/all_gather | solution.py:37
  113.4 46.8 %copy-start.2 = (bf16[32,8,640]{2,0,1:T(8,128)(2,1)S(1)}, bf16[32,8,640]{2,0,1:T(8,128)(2,1)}, u32[]{:S(2)}) copy-start(bf16[32,8,640]{2,0,1:T(8,128)(2,1)} %copy-done.1) | copy-start | bytes 983044
  157.3 116.6 %copy-start.4 = (f32[256,128]{1,0:T(8,128)}, f32[256,128]{1,0:T(8,128)S(1)}, u32[]{:S(2)}) copy-start(f32[256,128]{1,0:T(8,128)S(1)} %get-tuple-element.362) | copy-start | bytes 393220
  305.4 18.6 %copy-start.3 = (bf16[32,2560]{1,0:T(8,128)(2,1)S(1)}, bf16[32,2560]{1,0:T(8,128)(2,1)}, u32[]{:S(2)}) copy-start(bf16[32,2560]{1,0:T(8,128)(2,1)} %param.12) | copy-start | bytes 491524
  309.1 14.7 %all-to-all-start.5 = ((bf16[8,2,160]{2,1,0:T(2,128)(2,1)}), bf16[8,2,160]{2,1,0:T(2,128)(2,1)S(1)}, u32[]{:S(2)}, u32[]{:S(2)}) async-start(bf16[8,2,160]{2,1,0:T(2,128)(2,1)} %reshape.401), calls=%async_computation.5 | async-start | bytes 16384 | tf_op jit(solution)/shard_map/all_to_all | solution.py:194
  316.2 37.1 %reduce-scatter.4.cloned.1.call-start = ((), (), s32[]{:S(2)}) async-start(), calls=%async_computation.9 | async-start | bytes 147456
  317.0 435.7 %all-reduce.4.cloned.1.call-start = ((), (), s32[]{:S(2)}) async-start(), calls=%async_computation.10 | async-start | bytes 6881280 | tf_op jit(solution)/shard_map/psum | solution.py:213
  325.2 30.8 %copy-start.51 = (f32[80]{0:T(128)S(1)}, f32[80]{0:T(128)}, u32[]{:S(2)}) copy-start(f32[80]{0:T(128)} %param.19) | copy-start | bytes 964
  325.2 31.1 %copy-start.11 = (bf16[512,256]{1,0:T(8,128)(2,1)S(1)}, bf16[512,256]{1,0:T(8,128)(2,1)}, u32[]{:S(2)}) copy-start(bf16[512,256]{1,0:T(8,128)(2,1)} %copy-done.10) | copy-start | bytes 786436
  374.6 375.2 %copy-start.26 = (bf16[32,256]{1,0:T(8,128)(2,1)S(1)}, bf16[32,256]{1,0:T(8,128)(2,1)}, u32[]{:S(2)}) copy-start(bf16[32,256]{1,0:T(8,128)(2,1)} %reduce-scatter.4.cloned.1.call-done) | copy-start | bytes 49156
  374.6 375.7 %copy-start.6 = (bf16[2560,80]{0,1:T(8,128)(2,1)S(1)}, bf16[2560,80]{0,1:T(8,128)(2,1)}, u32[]{:S(2)}) copy-start(bf16[2560,80]{0,1:T(8,128)(2,1)} %param.16) | copy-start | bytes 1228804
  377.2 19.1 %all-to-all-start.2 = ((bf16[8,32,640]{2,1,0:T(8,128)(2,1)}), bf16[8,32,640]{2,1,0:T(8,128)(2,1)S(1)}, u32[]{:S(2)}, u32[]{:S(2)}) async-start(bf16[8,32,640]{2,1,0:T(8,128)(2,1)} %get-tuple-element.546), calls=%async_computation.2 | async-start | bytes 655360 | tf_op jit(solution)/shard_map/all_to_all | solution.py:192
  396.3 355.7 %all-to-all-start.4 = ((bf16[8,32,640]{2,1,0:T(8,128)(2,1)}), bf16[8,32,640]{2,1,0:T(8,128)(2,1)S(1)}, u32[]{:S(2)}, u32[]{:S(2)}) async-start(bf16[8,32,640]{2,1,0:T(8,128)(2,1)} %get-tuple-element.545), calls=%async_computation.4 | async-start | bytes 655360 | tf_op jit(solution)/shard_map/all_to_all | solution.py:193
  (37 other events, 244.3 us)
Sparse Core Ops, SparseCore 0:
  98.2 47.6 all-gather.6
  148.9 60.7 all-gather.8
  320.1 33.1 reduce-scatter.3
  360.2 238.0 all-reduce.3
